TPU v7x, 512 devices: a whole 4x4x16 slice. The times are simulated.
512 devices in a mesh: row: 16 (over y, z_lo), col: 32 (over z_hi, x, core).
Axes of the slice: x: 4, y: 4, z: 16 (z_hi: 4, z_lo: 4; z = z_hi * 4 + z_lo), core: 2. Of those that a mesh axis runs over, the one named last changes fastest.
Arguments:
- eigenbasis: float32 [18432, 18432], P('row', 'col'), may hold values from -0.078125 to 0.078125
- eigenvalues: float32 [18432], P('col'), may hold values from 0.02 to 2
- queries: float32 [18432, 256], P('row'), may hold values from -6 to 6
- activations: bfloat16 [16384, 18432], P('row', 'col'), may hold values from -0.078125 to 0.078125
Outputs:
- scores: float32 [16384, 256], P(('row', 'col'))
All inputs are finite; a program needn't handle non-finite values.
Results may differ from a plain program's by a relative error of at most 0.0029.
Values may be sent and summed in bfloat16 or wider, within the bound.
A program may use at most 64 MiB of HBM per device.

v0:
```python
import jax
import jax.numpy as jnp
from jax import lax
from jax.sharding import PartitionSpec as P

damping = 0.1


def from_root(block, axis, holder):
    block = jnp.where(lax.axis_index(axis) == holder, block, jnp.zeros_like(block))
    return lax.psum(block, axis)


def per_device(eigenbasis, eigenvalues, queries, activations):
    rows_here, cols_here = eigenbasis.shape
    row_pos = lax.axis_index("row")
    col_pos = lax.axis_index("col")
    row_share = cols_here // lax.axis_size("row")
    rotated = lax.psum_scatter(
        lax.dot_general(
            eigenbasis,
            queries,
            (((0,), (0,)), ((), ())),
            precision=lax.Precision.HIGHEST,
            preferred_element_type=jnp.float32,
        ),
        "row",
        scatter_dimension=0,
        tiled=True,
    )
    local_values = lax.dynamic_slice_in_dim(eigenvalues, row_pos * row_share, row_share, 0)
    scaled_part = rotated / (local_values[:, None] + damping)
    scaled = lax.all_gather(scaled_part, "row", axis=0, tiled=True)
    owner_row = col_pos * cols_here // rows_here
    offset = col_pos * cols_here - owner_row * rows_here
    row_block = lax.psum(
        jnp.dot(
            eigenbasis, scaled, precision=lax.Precision.HIGHEST, preferred_element_type=jnp.float32
        ),
        "col",
    ).astype(jnp.bfloat16)
    own_slice = lax.dynamic_slice_in_dim(row_block, offset, cols_here, 0)
    precond = from_root(own_slice, "row", owner_row)
    return lax.psum_scatter(
        jnp.dot(activations, precond, preferred_element_type=jnp.float32),
        "col",
        scatter_dimension=0,
        tiled=True,
    )


def solution(mesh):
    placed = (P("row", "col"), P("col"), P("row", None), P("row", "col"))
    return jax.shard_map(
        per_device, mesh=mesh, in_specs=placed, out_specs=P(("row", "col"), None), check_vma=False
    )
```

profile of v0, /device:TPU:1, one launch (start us, length us, event | category | flops | bytes accessed | tf_op | source)
XLA Modules:
  0.0 593.2 jit_solution(6137952195494885036)
XLA Ops:
  6.5 0.0 copy-start
  6.5 0.0 all-reduce.5.cloned.1.call-start
  6.5 1.7 copy-done
  8.3 3.7 fusion.3
  12.0 45.4 %fusion = f32[40,256]{1,0:T(8,128)S(1)} fusion(f32[576,256]{1,0:T(8,128)S(1)} %fusion.3), kind=kCustom, calls=%all-reduce-scatter | all-reduce-scatter fusion | flops 163841 | bytes 632832
  57.4 1.3 collective-permute-start
  58.7 1.3 collective-permute-start.1
  60.0 0.8 dynamic-slice_add_fusion
  60.8 1.3 dynamic-slice.4
  62.7 0.0 collective-permute-done.1
  62.7 0.0 collective-permute-done
  62.7 0.3 concatenate
  63.0 0.1 fusion.2
  63.1 37.9 %all-gather = f32[16,36,256]{2,1,0:T(8,128)S(1)} all-gather(f32[1,36,256]{2,1,0:T(8,128)S(1)} %fusion.2), channel_id=1, replica_groups=mesh['row'=16,'col'=32] {'row'}, dimensions={0}, use_global_device_ids=true | all-gather | bytes 626688 | tf_op jit(solution)/shard_map/all_gather | solution.py:33
  101.0 0.9 reshape.3
  101.9 5.3 convolution_bitcast_fusion
  107.2 193.8 %all-reduce.6 = bf16[1152,256]{0,1:T(8,128)(2,1)S(1)} all-reduce(f32[1152,256]{0,1:T(8,128)} %convolution_bitcast_fusion), channel_id=1, replica_groups=mesh['row'=16,'col'=32] {'col'}, use_global_device_ids=true, to_apply=%region_1.2 | all-reduce | flops 294912 | bytes 1769472 | tf_op jit(solution)/shard_map/psum | solution.py:36
  301.0 0.9 fusion.1
  301.9 0.0 all-reduce.5.cloned.1.call-update
  301.9 0.0 reduce-scatter.6.cloned.1.call-start
  302.0 158.9 %all-reduce.5.cloned.1.call-done = bf16[576,256]{0,1:T(8,128)(2,1)} async-done(((bf16[576,256]{0,1:T(8,128)(2,1)}), bf16[576,256]{0,1:T(8,128)(2,1)}) %all-reduce.5.cloned.1.call-update) | async-done | bytes 294928 | tf_op jit(solution)/shard_map/psum | solution.py:11
  460.9 2.9 convolution_bitcast_fusion.1
  463.8 2.6 copy.8
  466.4 0.0 reduce-scatter.6.cloned.1.call-update
  466.4 120.0 %reduce-scatter.6.cloned.1.call-done = f32[32,256]{1,0:T(8,128)} async-done(((f32[1024,256]{1,0:T(8,128)}), f32[32,256]{1,0:T(8,128)}) %reduce-scatter.6.cloned.1.call-update) | async-done | bytes 32784 | tf_op jit(solution)/shard_map/reduce_scatter | solution.py:44
  (1 shorter events, 0.0 us)
Async XLA Ops:
  6.5 1.8 copy-start
  6.5 454.3 %all-reduce.5.cloned.1.call-start = ((), (), s32[]{:S(2)}) async-start(), calls=%async_computation.1 | async-start | bytes 655360 | tf_op jit(solution)/shard_map/psum | solution.py:11
  57.4 5.3 collective-permute-start
  58.7 4.0 collective-permute-start.1
  301.9 284.5 %reduce-scatter.6.cloned.1.call-start = ((), (), s32[]{:S(2)}) async-start(), calls=%async_computation.2 | async-start | bytes 1081344 | tf_op jit(solution)/shard_map/reduce_scatter | solution.py:44
Sparse Core Ops, SparseCore 0:
  302.0 158.7 all-reduce.4
  466.6 119.7 reduce-scatter.5
where the time goes:
time: 595 us; the launch traced here: 593 us
  waiting for transfers between devices  279 us (47%)
  blocking collectives  277 us (47%)
  between operations  14.1 us (2%)
  matrix products  12 us (2%)
  local copies, waits for them, and re-layouts  6.79 us (1%)
    psum x1, blocking collectives, per_device(): lax.psum(jnp.dot(eigenbasis, scaled, precision=lax.Precision.HIGHEST, pre...  194 us
    psum x1, waiting for transfers between devices, from_root(): return lax.psum(block, axis)  159 us
    reduce_scatter x1, waiting for transfers between devices, per_device(): lax.psum_scatter(jnp.dot(activations, precond, preferred_element_type=jnp...  120 us
    unnamed x1, blocking collectives  45.4 us
    all_gather x1, blocking collectives, per_device(): scaled = lax.all_gather(scaled_part, 'row', axis=0, tiled=True)  37.9 us
  transfers between devices with their start and end apart: 4, of which 2 were waited for; matrix products, arithmetic and copies ran while one was open for 0% of the time, Pallas kernels for 0%

commit v1 on v0

v1 whole, which is shorter than its diff:
```python
import functools

import jax
import jax.numpy as jnp
from jax import lax
from jax.experimental import pallas as pl
from jax.experimental.pallas import tpu as pltpu
from jax.sharding import PartitionSpec as P

damping = 0.1
MESH = pl.DeviceIdType.MESH
f32, bf16 = jnp.float32, jnp.bfloat16
CHUNKS = 2
QC = 128
COLS = 576
WIN = 640


def halves(v):
    hi = v.astype(bf16)
    return hi, (v - hi.astype(f32)).astype(bf16)


def dot(a, b):
    return jnp.dot(a, b, preferred_element_type=f32)


def kernel(
    et_hbm, ev_ref, q_hbm, at_hbm, out_ref,
    et_v, q_v, at_v, eh, el, rot, act,
    ry_tx, ry_rx, rz_tx, rz_rx, st,
    pk_tx, pk_rx, px_tx, px_rx, pz_tx, pz_rx, pm, pc_rx, pc,
    sk_tx, sk_own, sk_rx, sx_tx, sx_own, sx_rx, sz_tx, sz_own, sz_rx,
    load_sem, quad_tx, quad_rx, pair_tx, pair_rx, all_tx, all_rx,
):
    row, col = lax.axis_index("row"), lax.axis_index("col")
    y, zl = row // 4, row % 4
    zh, x, k = col // 8, (col // 2) % 4, col % 2

    def device(y=y, zl=zl, zh=zh, x=x, k=k):
        return (y * 4 + zl, zh * 8 + x * 2 + k)

    turned = device(y=zh, zl=x, zh=y, x=zl)
    stays = (x == zl) & (zh == y)

    loads = [
        pltpu.make_async_copy(q_hbm, q_v, load_sem.at[0]),
        pltpu.make_async_copy(et_hbm, et_v, load_sem.at[1]),
        pltpu.make_async_copy(at_hbm, at_v.at[pl.ds(pl.multiple_of(k * 64, 64), COLS)], load_sem.at[2]),
    ]
    for load in loads:
        load.start()

    barrier = pltpu.get_barrier_semaphore()

    def greet(who):
        pl.semaphore_signal(barrier, inc=1, device_id=who, device_id_type=MESH)

    row_peers = []
    for dy in range(4):
        for dz in range(4):
            if dy or dz:
                row_peers.append(((y + dy) % 4, (zl + dz) % 4))
    for py, pz in row_peers:
        greet(device(y=py, zl=pz))
    greet(device(k=1 - k))
    for d in range(1, 4):
        greet(device(x=(x + d) % 4))
        greet(device(zh=(zh + d) % 4))

    @pl.when(jnp.logical_not(stays))
    def _():
        greet(turned)

    at_v[pl.ds(pl.multiple_of((1 - k) * COLS, 64), 64), :] = jnp.zeros((64, 1024), bf16)

    loads[0].wait()
    qh, ql = halves(q_v[...])
    loads[1].wait()
    tile = 288
    for i in range(COLS // tile):
        rows = pl.ds(i * tile, tile)
        h, l = halves(et_v[rows, :])
        eh[rows, :] = h
        el[rows, :] = l
        rot[rows, :] = dot(h, qh) + dot(h, ql) + dot(l, qh)

    pl.semaphore_wait(barrier, 22 + jnp.where(stays, 0, 1))

    sent = []

    def send(src, dst, tx, rx, who):
        copy = pltpu.make_async_remote_copy(
            src_ref=src, dst_ref=dst, send_sem=tx, recv_sem=rx, device_id=who, device_id_type=MESH
        )
        copy.start()
        sent.append(copy)
        return copy

    def quad(stage, ch, source, target, axis, at):
        copies = []
        for d in range(1, 4):
            to = (at + d) % 4
            copies.append(
                send(source(to), target(d - 1), quad_tx.at[stage, ch, d - 1], quad_rx.at[stage, ch, d - 1],
                     device(**{axis: to}))
            )
        return copies

    def chunk(ch):
        lanes = slice(ch * QC, (ch + 1) * QC)
        ry_tx[ch] = rot[:, lanes].T.reshape(4, 32, COLS)
        copies = quad(0, ch, lambda to: ry_tx.at[ch, to], lambda s: ry_rx.at[ch, s], "y", y)
        yield
        for copy in copies:
            copy.wait_recv()
        total = ry_tx[ch, y] + ry_rx[ch, 0] + ry_rx[ch, 1] + ry_rx[ch, 2]
        rz_tx[ch] = total.reshape(4, 8, COLS)
        copies = quad(1, ch, lambda to: rz_tx.at[ch, to], lambda s: rz_rx.at[ch, s], "zl", zl)
        yield
        for copy in copies:
            copy.wait_recv()
        total = rz_tx[ch, zl] + rz_rx[ch, 0] + rz_rx[ch, 1] + rz_rx[ch, 2]
        st[ch, y, zl] = total / (ev_ref[...] + damping)
        copies = quad(2, ch, lambda to: st.at[ch, y, zl], lambda s: st.at[ch, y, zl], "zl", zl)
        yield
        for copy in copies:
            copy.wait_recv()
        copies = quad(3, ch, lambda to: st.at[ch, y], lambda s: st.at[ch, y], "y", y)
        yield
        for copy in copies:
            copy.wait_recv()
        sh, sl = halves(st[ch].reshape(QC, COLS))
        both = jnp.concatenate([sh, sl], axis=0)

        def window(at):
            cols = pl.ds(pl.multiple_of(at * 512, 128), WIN)
            wide = dot(both, eh[:, cols])
            return wide[:QC] + wide[QC:] + dot(sh, el[:, cols])

        pk_tx[ch] = window(1 - k)
        copy = send(pk_tx.at[ch], pk_rx.at[ch], pair_tx.at[0, ch], pair_rx.at[0, ch], device(k=1 - k))
        own = window(k)
        copy.wait_recv()
        px_tx[ch] = (own + pk_rx[ch]).reshape(4, 32, WIN)
        copies = quad(4, ch, lambda to: px_tx.at[ch, to], lambda s: px_rx.at[ch, s], "x", x)
        yield
        for copy in copies:
            copy.wait_recv()
        total = px_tx[ch, x] + px_rx[ch, 0] + px_rx[ch, 1] + px_rx[ch, 2]
        pz_tx[ch] = total.reshape(4, 8, WIN)
        copies = quad(5, ch, lambda to: pz_tx.at[ch, to], lambda s: pz_rx.at[ch, s], "zh", zh)
        yield
        for copy in copies:
            copy.wait_recv()
        total = pz_tx[ch, zh] + pz_rx[ch, 0] + pz_rx[ch, 1] + pz_rx[ch, 2]
        pm[ch] = jnp.concatenate([total[:, :384], total[:, 256:]], axis=0).astype(bf16)
        moved = pltpu.make_async_remote_copy(
            src_ref=pm.at[ch], dst_ref=pc_rx.at[ch, x, zh], send_sem=pair_tx.at[1, ch], recv_sem=pair_rx.at[1, ch],
            device_id=turned, device_id_type=MESH,
        )

        @pl.when(jnp.logical_not(stays))
        def _():
            moved.start()

        @pl.when(stays)
        def _():
            pc_rx[ch, x, zh] = pm[ch]

        yield

        @pl.when(jnp.logical_not(stays))
        def _():
            moved.wait()

        copies = []
        for n, (py, pz) in enumerate(row_peers):
            here = pc_rx.at[ch, zl, y]
            copies.append(send(here, here, all_tx.at[ch, n], all_rx.at[ch, n], device(y=py, zl=pz)))
        yield
        for copy in copies:
            copy.wait_recv()
        for a in range(4):
            for b in range(4):
                v = pc_rx[ch, a, b].astype(f32)
                rows = slice(32 * a + 8 * b, 32 * a + 8 * b + 8)
                pc[ch, rows, 0:384] = v[0:8]
                pc[ch, rows, 384:640] = v[8:16, 128:384]
        precond = pc[ch].astype(bf16)

        def scores(half):
            tokens = act[half].reshape(512, WIN)
            return lax.dot_general(tokens, precond, (((1,), (1,)), ((), ())), preferred_element_type=f32)

        sk_tx[ch] = scores(1 - k)
        copy = send(sk_tx.at[ch], sk_rx.at[ch], pair_tx.at[2, ch], pair_rx.at[2, ch], device(k=1 - k))
        own = scores(k)
        copy.wait_recv()
        total = (own + sk_rx[ch]).reshape(4, 128, QC)
        sx_own[ch] = total
        sx_tx[ch] = total.astype(bf16)
        copies = quad(6, ch, lambda to: sx_tx.at[ch, to], lambda s: sx_rx.at[ch, s], "x", x)
        yield
        for copy in copies:
            copy.wait_recv()
        total = sx_own[ch, x]
        for s in range(3):
            total = total + sx_rx[ch, s].astype(f32)
        total = total.reshape(4, 32, QC)
        sz_own[ch] = total
        sz_tx[ch] = total.astype(bf16)
        copies = quad(7, ch, lambda to: sz_tx.at[ch, to], lambda s: sz_rx.at[ch, s], "zh", zh)
        yield
        for copy in copies:
            copy.wait_recv()
        total = sz_own[ch, zh]
        for s in range(3):
            total = total + sz_rx[ch, s].astype(f32)
        out_ref[:, lanes] = total

    running = [chunk(ch) for ch in range(CHUNKS)]
    turn = 0
    while running:
        for one in list(running):
            try:
                next(one)
            except StopIteration:
                running.remove(one)
        if turn == 0:
            loads[2].wait()
            for t in range(8):
                block = at_v[:, t * 128 : (t + 1) * 128].T
                for i in range(4):
                    c = 4 * t + i
                    act[c % 2, (c // 2) % 4, c // 8] = block[32 * i : 32 * i + 32]
        turn += 1
    for copy in sent:
        copy.wait_send()


def per_device(eigenbasis, eigenvalues, queries, activations):
    n = CHUNKS
    dma = pltpu.SemaphoreType.DMA
    V = pltpu.VMEM
    any_space = pl.BlockSpec(memory_space=pl.ANY)
    vmem = pl.BlockSpec(memory_space=V)
    return pl.pallas_call(
        kernel,
        out_shape=jax.ShapeDtypeStruct((32, 256), f32),
        in_specs=[any_space, vmem, any_space, any_space],
        out_specs=vmem,
        scratch_shapes=[
            V((COLS, 1152), f32), V((1152, 256), f32), V((WIN, 1024), bf16),
            V((COLS, 1152), bf16), V((COLS, 1152), bf16), V((COLS, 256), f32), V((2, 4, 4, 32, WIN), bf16),
            V((n, 4, 32, COLS), f32), V((n, 3, 32, COLS), f32), V((n, 4, 8, COLS), f32), V((n, 3, 8, COLS), f32),
            V((n, 4, 4, 8, COLS), f32),
            V((n, QC, WIN), f32), V((n, QC, WIN), f32), V((n, 4, 32, WIN), f32), V((n, 3, 32, WIN), f32),
            V((n, 4, 8, WIN), f32), V((n, 3, 8, WIN), f32), V((n, 16, 384), bf16), V((n, 4, 4, 16, 384), bf16),
            V((n, QC, WIN), f32),
            V((n, 512, QC), f32), V((1, 8, 128), f32), V((n, 512, QC), f32),
            V((n, 4, 128, QC), bf16), V((n, 4, 128, QC), f32), V((n, 3, 128, QC), bf16),
            V((n, 4, 32, QC), bf16), V((n, 4, 32, QC), f32), V((n, 3, 32, QC), bf16),
            dma((3,)), dma((8, n, 3)), dma((8, n, 3)), dma((3, n)), dma((3, n)), dma((n, 15)), dma((n, 15)),
        ],
        compiler_params=pltpu.CompilerParams(
            collective_id=1, has_side_effects=True, vmem_limit_bytes=56 * 1024 * 1024
        ),
    )(eigenbasis.T, eigenvalues.reshape(1, -1), queries, activations.T)


def solution(mesh):
    placed = (P("row", "col"), P("col"), P("row", None), P("row", "col"))
    return jax.shard_map(
        per_device, mesh=mesh, in_specs=placed, out_specs=P(("row", "col"), None), check_vma=False
    )
```

time: 595 us -> 91.6 us (0.15)
  waiting for transfers between devices: 279 us -> 0 us
  blocking collectives: 277 us -> 0 us
  Pallas kernels: 0 us -> 87.8 us
  between operations: 14.1 us -> 0.01 us
  matrix products: 12 us -> 0 us
    psum x1 -> x0, blocking collectives: 194 us -> none  [per_device(): lax.psum(jnp.dot(eigenbasis, scaled, precision=lax.Precision.HIGHEST, pre...]
    psum x1 -> x0, waiting for transfers between devices: 159 us -> none  [from_root(): return lax.psum(block, axis)]
    reduce_scatter x1 -> x0, waiting for transfers between devices: 120 us -> none  [per_device(): lax.psum_scatter(jnp.dot(activations, precond, preferred_element_type=jnp...]
    pallas_call x0 -> x1, Pallas kernels: none -> 87.8 us  [per_device(): pl.pallas_call(kernel, out_shape=jax.ShapeDtypeStruct((32, 256), f32), in...]
    unnamed x1 -> x0, blocking collectives: 45.4 us -> none
    all_gather x1 -> x0, blocking collectives: 37.9 us -> none  [per_device(): scaled = lax.all_gather(scaled_part, 'row', axis=0, tiled=True)]
    dot_general x3 -> x0, matrix products: 12 us -> none  [the longest x1 5.29 us: per_device(): jnp.dot(eigenbasis, scaled, precision=lax.Precision.HIGHEST, preferred_el...]
  transfers between devices with their start and end apart: 4 -> 0, of which waited for: 2 -> 0; matrix products, arithmetic and copies ran while one was open for 0% -> 0% of each run, Pallas kernels for 0% -> 0%
where the time goes in v1:
time: 91.6 us; the launch traced here: 90.4 us
  Pallas kernels  87.8 us (96%)
  local copies, waits for them, and re-layouts  2.64 us (3%)
    pallas_call x1, Pallas kernels, per_device(): pl.pallas_call(kernel, out_shape=jax.ShapeDtypeStruct((32, 256), f32), in...  87.8 us

profile of v1, /device:TPU:1, one launch (start us, length us, event | category | flops | bytes accessed | tf_op | source)
XLA Modules:
  0.0 90.4 jit_solution(13612808582659341385)
XLA Ops:
  0.0 1.3 %reshape.3.ev_ref = f32[1,576]{1,0:T(1,128)} reshape(f32[576]{0:T(1024)} %param.5) | data formatting | bytes 4608 | tf_op jit(solution)/shard_map/reshape | solution.py:269
  1.3 87.8 %shard_map.46 = f32[32,256]{1,0:T(8,128)} custom-call(f32[576,1152]{1,0:T(8,128)} %bitcast.2, f32[1,576]{1,0:T(1,128)} %reshape.3.ev_ref, f32[1152,256]{1,0:T(8,128)} %q_hbm.1, bf16[576,1024]{1,0:T(8,128)(2,1)} %bitcast.3), custom_call_target="tpu_custom_call" | custom-call | tf_op jit(solution)/shard_map/pallas_call | solution.py:248
  89.0 1.4 %copy.6 = f32[32,256]{1,0:T(8,128)} copy(f32[32,256]{1,0:T(8,128)} %shard_map.46) | data formatting | bytes 65536

commit v2 on v1

v2 whole, which is shorter than its diff:
```python
import functools

import jax
import jax.numpy as jnp
from jax import lax
from jax.experimental import pallas as pl
from jax.experimental.pallas import tpu as pltpu
from jax.sharding import PartitionSpec as P

damping = 0.1
MESH = pl.DeviceIdType.MESH
f32, bf16 = jnp.float32, jnp.bfloat16
CHUNKS = 2
QC = 128
COLS = 576
EIG = ((0, 256), (256, 576))
WIDE = ((0, 256), (256, 640))
PACK = (128, 256)
WIN = 640


def halves(v):
    hi = v.astype(bf16)
    return hi, (v - hi.astype(f32)).astype(bf16)


def dot(a, b):
    return jnp.dot(a, b, preferred_element_type=f32)


def kernel(
    et_hbm, ev_ref, q_hbm, at_hbm, out_ref,
    et_v, q_v, at_v, eh, el, rot, act,
    ry_tx, ry_rx, rz_tx, rz_rx, st,
    pk_tx, pk_rx, px_tx, px_rx, pz_tx, pz_rx, pm, pc_rx, pc,
    sk_tx, sk_rx, sx_tx, sx_own, sx_rx, sz_tx, sz_own, sz_rx,
    load_sem, quad_tx, quad_rx, pair_tx, pair_rx, turn_tx, turn_rx, all_tx, all_rx,
):
    row, col = lax.axis_index("row"), lax.axis_index("col")
    y, zl = row // 4, row % 4
    zh, x, k = col // 8, (col // 2) % 4, col % 2

    def device(y=y, zl=zl, zh=zh, x=x, k=k):
        return (y * 4 + zl, zh * 8 + x * 2 + k)

    turned = device(y=zh, zl=x, zh=y, x=zl)
    stays = (x == zl) & (zh == y)

    loads = [
        pltpu.make_async_copy(q_hbm, q_v, load_sem.at[0]),
        pltpu.make_async_copy(et_hbm, et_v, load_sem.at[1]),
        pltpu.make_async_copy(at_hbm, at_v.at[pl.ds(pl.multiple_of(k * 64, 64), COLS)], load_sem.at[2]),
    ]
    loads[0].start()
    loads[1].start()

    barrier = pltpu.get_barrier_semaphore()

    def greet(who):
        pl.semaphore_signal(barrier, inc=1, device_id=who, device_id_type=MESH)

    row_peers = []
    for dy in range(4):
        for dz in range(4):
            if dy or dz:
                row_peers.append(((y + dy) % 4, (zl + dz) % 4))
    for py, pz in row_peers:
        greet(device(y=py, zl=pz))
    greet(device(k=1 - k))
    for d in range(1, 4):
        greet(device(x=(x + d) % 4))
        greet(device(zh=(zh + d) % 4))

    @pl.when(jnp.logical_not(stays))
    def _():
        greet(turned)

    loads[2].start()
    at_v[pl.ds(pl.multiple_of((1 - k) * COLS, 64), 64), :] = jnp.zeros((64, 1024), bf16)

    loads[0].wait()
    qh, ql = halves(q_v[...])
    loads[1].wait()
    for lo, hi in EIG:
        h, l = halves(et_v[lo:hi, :])
        eh[lo:hi, :] = h
        el[lo:hi, :] = l
        rot[lo:hi, :] = dot(h, qh) + dot(h, ql) + dot(l, qh)

    pl.semaphore_wait(barrier, 22 + jnp.where(stays, 0, 1))

    sent = []

    def send(src, dst, tx, rx, who):
        copy = pltpu.make_async_remote_copy(
            src_ref=src, dst_ref=dst, send_sem=tx, recv_sem=rx, device_id=who, device_id_type=MESH
        )
        copy.start()
        sent.append(copy)
        return copy

    def quad(stage, ch, part, source, target, axis, at):
        copies = []
        for d in range(1, 4):
            to = (at + d) % 4
            copies.append(
                send(source(to), target(d - 1), quad_tx.at[stage, ch, part, d - 1], quad_rx.at[stage, ch, part, d - 1],
                     device(**{axis: to}))
            )
        return copies

    def arrive(copies):
        for copy in copies:
            copy.wait_recv()

    def rotate(ch, p):
        lanes = slice(ch * QC, (ch + 1) * QC)
        lo, hi = EIG[p]
        tx, rx, tz, rz, s = ry_tx[p], ry_rx[p], rz_tx[p], rz_rx[p], st[p]
        tx[ch] = rot[lo:hi, lanes].T.reshape(4, 32, hi - lo)
        copies = quad(0, ch, p, lambda to: tx.at[ch, to], lambda i: rx.at[ch, i], "y", y)
        yield
        arrive(copies)
        total = tx[ch, y] + rx[ch, 0] + rx[ch, 1] + rx[ch, 2]
        tz[ch] = total.reshape(4, 8, hi - lo)
        copies = quad(1, ch, p, lambda to: tz.at[ch, to], lambda i: rz.at[ch, i], "zl", zl)
        yield
        arrive(copies)
        total = tz[ch, zl] + rz[ch, 0] + rz[ch, 1] + rz[ch, 2]
        s[ch, y, zl] = total / (ev_ref[...].reshape(1, COLS)[:, lo:hi] + damping)
        copies = quad(2, ch, p, lambda to: s.at[ch, y, zl], lambda i: s.at[ch, y, zl], "zl", zl)
        yield
        arrive(copies)
        copies = quad(3, ch, p, lambda to: s.at[ch, y], lambda i: s.at[ch, y], "y", y)
        yield
        arrive(copies)

    def expand(ch, state):
        pieces = []
        for p, (lo, hi) in enumerate(EIG):
            sh, sl = halves(st[p][ch].reshape(QC, hi - lo))
            pieces.append((lo, hi, sh, jnp.concatenate([sh, sl], axis=0)))

        def window(at, p):
            first, last = WIDE[p]
            cols = pl.ds(pl.multiple_of(at * 512 + first, 128), last - first)
            total = None
            for lo, hi, sh, both in pieces:
                wide = dot(both, eh[lo:hi, cols])
                term = wide[:QC] + wide[QC:] + dot(sh, el[lo:hi, cols])
                total = term if total is None else total + term
            return total

        for p in range(2):
            pk_tx[p][ch] = window(1 - k, p)
            state[ch, p] = send(
                pk_tx[p].at[ch], pk_rx[p].at[ch], pair_tx.at[p, ch], pair_rx.at[p, ch], device(k=1 - k)
            )
        for p in range(2):
            first, last = WIDE[p]
            px_tx[p][ch] = window(k, p).reshape(4, 32, last - first)

    def collect(ch, p, state):
        first, last = WIDE[p]
        width = last - first
        tx, rx, tz, rz = px_tx[p], px_rx[p], pz_tx[p], pz_rx[p]
        state[ch, p].wait_recv()
        tx[ch] = tx[ch] + pk_rx[p][ch].reshape(4, 32, width)
        copies = quad(4, ch, p, lambda to: tx.at[ch, to], lambda i: rx.at[ch, i], "x", x)
        yield
        arrive(copies)
        total = tx[ch, x] + rx[ch, 0] + rx[ch, 1] + rx[ch, 2]
        tz[ch] = total.reshape(4, 8, width)
        copies = quad(5, ch, p, lambda to: tz.at[ch, to], lambda i: rz.at[ch, i], "zh", zh)
        yield
        arrive(copies)
        total = tz[ch, zh] + rz[ch, 0] + rz[ch, 1] + rz[ch, 2]
        pm[p][ch] = jnp.concatenate([total[:, : PACK[p]], total[:, width - PACK[p] :]], axis=0).astype(bf16)
        moved = pltpu.make_async_remote_copy(
            src_ref=pm[p].at[ch], dst_ref=pc_rx[p].at[ch, x, zh], send_sem=turn_tx.at[p, ch],
            recv_sem=turn_rx.at[p, ch], device_id=turned, device_id_type=MESH,
        )

        @pl.when(jnp.logical_not(stays))
        def _():
            moved.start()

        @pl.when(stays)
        def _():
            pc_rx[p][ch, x, zh] = pm[p][ch]

        yield

        @pl.when(jnp.logical_not(stays))
        def _():
            moved.wait()

        copies = []
        here = pc_rx[p].at[ch, zl, y]
        for n, (py, pz) in enumerate(row_peers):
            copies.append(send(here, here, all_tx.at[ch, p, n], all_rx.at[ch, p, n], device(y=py, zl=pz)))
        yield
        arrive(copies)
        for a in range(4):
            for b in range(4):
                v = pc_rx[p][ch, a, b].astype(f32)
                rows = slice(32 * a + 8 * b, 32 * a + 8 * b + 8)
                pc[ch, rows, first : first + PACK[p]] = v[0:8]
                pc[ch, rows, last - PACK[p] : last] = v[8:16]

    def score(ch, state):
        precond = pc[ch].astype(bf16)

        def scores(half):
            tokens = act[half].reshape(512, WIN)
            return lax.dot_general(tokens, precond, (((1,), (1,)), ((), ())), preferred_element_type=f32)

        sk_tx[ch] = scores(1 - k)
        state[ch] = send(sk_tx.at[ch], sk_rx.at[ch], pair_tx.at[2, ch], pair_rx.at[2, ch], device(k=1 - k))
        sx_own[ch] = scores(k).reshape(4, 128, QC)

    def finish(ch, state):
        lanes = slice(ch * QC, (ch + 1) * QC)
        state[ch].wait_recv()
        total = sx_own[ch] + sk_rx[ch].reshape(4, 128, QC)
        sx_own[ch] = total
        sx_tx[ch] = total.astype(bf16)
        copies = quad(6, ch, 0, lambda to: sx_tx.at[ch, to], lambda s: sx_rx.at[ch, s], "x", x)
        yield
        arrive(copies)
        total = sx_own[ch, x]
        for s in range(3):
            total = total + sx_rx[ch, s].astype(f32)
        total = total.reshape(4, 32, QC)
        sz_own[ch] = total
        sz_tx[ch] = total.astype(bf16)
        copies = quad(7, ch, 0, lambda to: sz_tx.at[ch, to], lambda s: sz_rx.at[ch, s], "zh", zh)
        yield
        arrive(copies)
        total = sz_own[ch, zh]
        for s in range(3):
            total = total + sz_rx[ch, s].astype(f32)
        out_ref[:, lanes] = total

    def step(streams):
        for one in streams:
            next(one, None)

    summed = {}
    first = [[rotate(ch, p) for p in range(2)] for ch in range(CHUNKS)]
    for stage in range(4):
        step(first[0] + first[1])
        if stage == 1:
            loads[2].wait()
            for t in range(8):
                block = at_v[:, t * 128 : (t + 1) * 128].T
                for i in range(4):
                    c = 4 * t + i
                    act[c % 2, (c // 2) % 4, c // 8] = block[32 * i : 32 * i + 32]
    for ch in range(CHUNKS):
        step(first[ch])
        expand(ch, summed)
    second = [[collect(ch, p, summed) for p in range(2)] for ch in range(CHUNKS)]
    for stage in range(4):
        step(second[0] + second[1])
    for ch in range(CHUNKS):
        step(second[ch])
        score(ch, summed)
    third = [finish(ch, summed) for ch in range(CHUNKS)]
    step(third)
    for copy in sent:
        copy.wait_send()
    sent.clear()
    step(third)
    step(third)
    for copy in sent:
        copy.wait_send()


def per_device(eigenbasis, eigenvalues, queries, activations):
    n = CHUNKS
    dma = pltpu.SemaphoreType.DMA
    V = pltpu.VMEM

    def parts(lanes, *lead):
        return [V((n, *lead, hi - lo), f32) for lo, hi in lanes]

    any_space = pl.BlockSpec(memory_space=pl.ANY)
    vmem = pl.BlockSpec(memory_space=V)
    return pl.pallas_call(
        kernel,
        out_shape=jax.ShapeDtypeStruct((32, 256), f32),
        in_specs=[any_space, vmem, any_space, any_space],
        out_specs=vmem,
        scratch_shapes=[
            V((COLS, 1152), f32), V((1152, 256), f32), V((WIN, 1024), bf16),
            V((COLS, 1152), bf16), V((COLS, 1152), bf16), V((COLS, 256), f32), V((2, 4, 4, 32, WIN), bf16),
            parts(EIG, 4, 32), parts(EIG, 3, 32), parts(EIG, 4, 8), parts(EIG, 3, 8), parts(EIG, 4, 4, 8),
            parts(WIDE, QC), parts(WIDE, QC), parts(WIDE, 4, 32), parts(WIDE, 3, 32), parts(WIDE, 4, 8),
            parts(WIDE, 3, 8), [V((n, 16, w), bf16) for w in PACK], [V((n, 4, 4, 16, w), bf16) for w in PACK],
            V((n, QC, WIN), f32),
            V((n, 512, QC), f32), V((n, 512, QC), f32),
            V((n, 4, 128, QC), bf16), V((n, 4, 128, QC), f32), V((n, 3, 128, QC), bf16),
            V((n, 4, 32, QC), bf16), V((n, 4, 32, QC), f32), V((n, 3, 32, QC), bf16),
            dma((3,)), dma((8, n, 2, 3)), dma((8, n, 2, 3)), dma((3, n)), dma((3, n)), dma((2, n)), dma((2, n)),
            dma((n, 2, 15)), dma((n, 2, 15)),
        ],
        compiler_params=pltpu.CompilerParams(
            collective_id=1, has_side_effects=True, vmem_limit_bytes=56 * 1024 * 1024
        ),
    )(eigenbasis.T, eigenvalues, queries, activations.T)


def solution(mesh):
    placed = (P("row", "col"), P("col"), P("row", None), P("row", "col"))
    return jax.shard_map(
        per_device, mesh=mesh, in_specs=placed, out_specs=P(("row", "col"), None), check_vma=False
    )
```

time: 91.6 us -> 88.1 us (0.962); the launches traced: 90.4 us -> 87.9 us
  Pallas kernels: 87.8 us -> 86.5 us
  local copies, waits for them, and re-layouts: 2.64 us -> 1.38 us
    pallas_call x1, Pallas kernels: 87.8 us -> 86.5 us  [per_device(): pl.pallas_call(kernel, out_shape=jax.ShapeDtypeStruct((32, 256), f32), in...]
    reshape x1 -> x0, local copies, waits for them, and re-layouts: 1.27 us -> none  [per_device(): eigenvalues.reshape(1, -1)]
where the time goes in v2:
time: 88.1 us; the launch traced here: 87.9 us
  Pallas kernels  86.5 us (98%)
  local copies, waits for them, and re-layouts  1.38 us (2%)
    pallas_call x1, Pallas kernels, per_device(): pl.pallas_call(kernel, out_shape=jax.ShapeDtypeStruct((32, 256), f32), in...  86.5 us

profile of v2, /device:TPU:1, one launch (start us, length us, event | category | flops | bytes accessed | tf_op | source)
XLA Modules:
  0.0 87.9 jit_solution(4302138881647944348)
XLA Ops:
  0.0 86.5 %shard_map.46 = f32[32,256]{1,0:T(8,128)} custom-call(f32[576,1152]{1,0:T(8,128)} %bitcast.2, f32[576]{0:T(1024)} %ev_ref.1, f32[1152,256]{1,0:T(8,128)} %q_hbm.1, bf16[576,1024]{1,0:T(8,128)(2,1)} %bitcast.3), custom_call_target="tpu_custom_call" | custom-call | tf_op jit(solution)/shard_map/pallas_call | solution.py:290
  86.5 1.4 %copy.6 = f32[32,256]{1,0:T(8,128)} copy(f32[32,256]{1,0:T(8,128)} %shard_map.46) | data formatting | bytes 65536

commit v3 on v2

v3 whole, which is shorter than its diff:
```python
import functools

import jax
import jax.numpy as jnp
from jax import lax
from jax.experimental import pallas as pl
from jax.experimental.pallas import tpu as pltpu
from jax.sharding import PartitionSpec as P

damping = 0.1
MESH = pl.DeviceIdType.MESH
f32, bf16 = jnp.float32, jnp.bfloat16
CHUNKS = 2
QC = 128
COLS = 576
EIG = ((0, 256), (256, 576))
WIDE = ((0, 256), (256, 640))
PACK = (128, 256)
WIN = 640


def halves(v):
    hi = v.astype(bf16)
    return hi, (v - hi.astype(f32)).astype(bf16)


def dot(a, b):
    return jnp.dot(a, b, preferred_element_type=f32)


def kernel(
    et_hbm, ev_ref, q_hbm, at_hbm, out_ref,
    et_v, q_v, at_v, eh, el, rot, act,
    ry_tx, ry_rx, rz_tx, rz_rx, st,
    pk_tx, pk_rx, px_tx, px_rx, pz_tx, pz_rx, pm, pc_rx, pc,
    sk_tx, sk_rx, sx_tx, sx_own, sx_rx, sz_tx, sz_own, sz_rx,
    load_sem, quad_tx, quad_rx, pair_tx, pair_rx, half_tx, half_rx, turn_tx, turn_rx, all_tx, all_rx,
):
    row, col = lax.axis_index("row"), lax.axis_index("col")
    y, zl = row // 4, row % 4
    zh, x, k = col // 8, (col // 2) % 4, col % 2

    def device(y=y, zl=zl, zh=zh, x=x, k=k):
        return (y * 4 + zl, zh * 8 + x * 2 + k)

    to_y = (y + x - zl + 6) % 4
    to_zl = (zh - y + 5 + zl // 2) % 4
    from_x = (x + y - zh + 6) % 4
    from_zh = (zh + zl + 7 - x // 2) % 4

    loads = [
        pltpu.make_async_copy(q_hbm, q_v, load_sem.at[0]),
        *(
            pltpu.make_async_copy(et_hbm.at[pl.ds(lo, hi - lo)], et_v.at[pl.ds(lo, hi - lo)], load_sem.at[1 + p])
            for p, (lo, hi) in enumerate(EIG)
        ),
        pltpu.make_async_copy(at_hbm, at_v.at[pl.ds(pl.multiple_of(k * 64, 64), COLS)], load_sem.at[3]),
    ]
    for load in loads[:3]:
        load.start()

    barrier = pltpu.get_barrier_semaphore()

    def greet(who):
        pl.semaphore_signal(barrier, inc=1, device_id=who, device_id_type=MESH)

    row_peers = [((y + dy) % 4, (zl + dz) % 4) for dz in (2, 1, 3, 0) for dy in (2, 1, 3, 0)][:15]
    greet(device(x=from_x, y=zh, zh=from_zh, zl=x))
    for d in (2, 1, 3):
        greet(device(zh=(zh + d) % 4))
    for py, pz in row_peers:
        greet(device(y=py, zl=pz))
    for d in (2, 1, 3):
        greet(device(x=(x + d) % 4))
    greet(device(k=1 - k))

    loads[3].start()
    at_v[pl.ds(pl.multiple_of((1 - k) * COLS, 64), 64), :] = jnp.zeros((64, 1024), bf16)

    loads[0].wait()
    qh, ql = halves(q_v[...])

    def rotated(p):
        lo, hi = EIG[p]
        loads[1 + p].wait()
        h, l = halves(et_v[lo:hi, :])
        eh[lo:hi, :] = h
        el[lo:hi, :] = l
        rot[lo:hi, :] = dot(h, qh) + dot(h, ql) + dot(l, qh)

    rotated(0)
    pl.semaphore_wait(barrier, 23)

    sent = []

    def send(src, dst, tx, rx, who):
        copy = pltpu.make_async_remote_copy(
            src_ref=src, dst_ref=dst, send_sem=tx, recv_sem=rx, device_id=who, device_id_type=MESH
        )
        copy.start()
        sent.append(copy)
        return copy

    def quad(stage, ch, part, source, target, axis, at):
        copies = []
        for d in range(1, 4):
            to = (at + d) % 4
            copies.append(
                send(source(to), target(d - 1), quad_tx.at[stage, ch, part, d - 1], quad_rx.at[stage, ch, part, d - 1],
                     device(**{axis: to}))
            )
        return copies

    def arrive(copies):
        for copy in copies:
            copy.wait_recv()

    def rotate(ch, p):
        lanes = slice(ch * QC, (ch + 1) * QC)
        lo, hi = EIG[p]
        near, far = (("zl", zl), ("y", y))[:: 1 if p == 0 else -1]
        tx, rx, tz, rz, s = ry_tx[p], ry_rx[p], rz_tx[p], rz_rx[p], st[p]
        i, j = near[1], far[1]
        tx[ch] = rot[lo:hi, lanes].T.reshape(4, 32, hi - lo)
        copies = quad(0, ch, p, lambda to: tx.at[ch, to], lambda n: rx.at[ch, n], *near)
        yield
        arrive(copies)
        total = tx[ch, i] + rx[ch, 0] + rx[ch, 1] + rx[ch, 2]
        tz[ch] = total.reshape(4, 8, hi - lo)
        copies = quad(1, ch, p, lambda to: tz.at[ch, to], lambda n: rz.at[ch, n], *far)
        yield
        arrive(copies)
        total = tz[ch, j] + rz[ch, 0] + rz[ch, 1] + rz[ch, 2]
        s[ch, i, j] = total / (ev_ref[...].reshape(1, COLS)[:, lo:hi] + damping)
        copies = quad(2, ch, p, lambda to: s.at[ch, i, j], lambda n: s.at[ch, i, j], *far)
        yield
        arrive(copies)
        copies = quad(3, ch, p, lambda to: s.at[ch, i], lambda n: s.at[ch, i], *near)
        yield
        arrive(copies)

    def expand(ch, part, state):
        lo, hi = EIG[part]
        sh, sl = halves(st[part][ch].reshape(QC, hi - lo))
        both = jnp.concatenate([sh, sl], axis=0)

        def window(at, p):
            first, last = WIDE[p]
            cols = pl.ds(pl.multiple_of(at * 512 + first, 128), last - first)
            wide = dot(both, eh[lo:hi, cols])
            return wide[:QC] + wide[QC:] + dot(sh, el[lo:hi, cols])

        for p in range(2):
            if part == 0:
                pk_tx[p][ch] = window(1 - k, p)
            else:
                pk_tx[p][ch] = pk_tx[p][ch] + window(1 - k, p)
                state[ch, p] = send(
                    pk_tx[p].at[ch], pk_rx[p].at[ch], pair_tx.at[p, ch], pair_rx.at[p, ch], device(k=1 - k)
                )
        for p in range(2):
            first, last = WIDE[p]
            own = window(k, p).reshape(4, 32, last - first)
            px_tx[p][ch] = own if part == 0 else px_tx[p][ch] + own

    def collect(ch, p, state):
        first, last = WIDE[p]
        width = last - first
        tx, rx, tz, rz = px_tx[p], px_rx[p], pz_tx[p], pz_rx[p]
        state[ch, p].wait_recv()
        tx[ch] = tx[ch] + pk_rx[p][ch].reshape(4, 32, width)
        copies = quad(4, ch, p, lambda to: tx.at[ch, to], lambda i: rx.at[ch, i], "x", x)
        yield
        arrive(copies)
        total = tx[ch, x] + rx[ch, 0] + rx[ch, 1] + rx[ch, 2]
        tz[ch] = total.reshape(4, 8, width)
        copies = quad(5, ch, p, lambda to: tz.at[ch, to], lambda i: rz.at[ch, i], "zh", zh)
        yield
        arrive(copies)
        total = tz[ch, zh] + rz[ch, 0] + rz[ch, 1] + rz[ch, 2]
        pm[p][ch] = jnp.concatenate([total[:, : PACK[p]], total[:, width - PACK[p] :]], axis=0).astype(bf16)
        moved = send(pm[p].at[ch], pc_rx[p].at[ch, x, zh], turn_tx.at[p, ch], turn_rx.at[p, ch],
                     device(x=zl, y=to_y, zh=y, zl=to_zl))
        yield
        moved.wait_recv()
        here = pc_rx[p].at[ch, from_x, from_zh]
        copies = []
        for n, (py, pz) in enumerate(row_peers):
            copies.append(send(here, here, all_tx.at[ch, p, n], all_rx.at[ch, p, n], device(y=py, zl=pz)))
        yield
        arrive(copies)
        for a in range(4):
            for b in range(4):
                v = pc_rx[p][ch, a, b].astype(f32)
                rows = slice(32 * a + 8 * b, 32 * a + 8 * b + 8)
                pc[ch, rows, first : first + PACK[p]] = v[0:8]
                pc[ch, rows, last - PACK[p] : last] = v[8:16]

    def score(ch, p, state):
        first, last = WIDE[p]
        precond = pc[ch, :, first:last].astype(bf16)

        def scores(core, half):
            tokens = act[core, half, :, :, :, first:last].reshape(256, last - first)
            return lax.dot_general(tokens, precond, (((1,), (1,)), ((), ())), preferred_element_type=f32)

        for h in range(2):
            if p == 0:
                sk_tx[ch, h] = scores(1 - k, h)
            else:
                sk_tx[ch, h] = sk_tx[ch, h] + scores(1 - k, h)
                state[ch, h] = send(
                    sk_tx.at[ch, h], sk_rx.at[ch, h], half_tx.at[ch, h], half_rx.at[ch, h], device(k=1 - k)
                )
        for h in range(2):
            own = scores(k, h).reshape(4, 64, QC)
            sx_own[ch, h] = own if p == 0 else sx_own[ch, h] + own

    def finish(ch, h, state):
        lanes = slice(ch * QC, (ch + 1) * QC)
        state[ch, h].wait_recv()
        total = sx_own[ch, h] + sk_rx[ch, h].reshape(4, 64, QC)
        sx_own[ch, h] = total
        sx_tx[ch, h] = total.astype(bf16)
        copies = quad(6, ch, h, lambda to: sx_tx.at[ch, h, to], lambda s: sx_rx.at[ch, h, s], "x", x)
        yield
        arrive(copies)
        total = sx_own[ch, h, x]
        for s in range(3):
            total = total + sx_rx[ch, h, s].astype(f32)
        total = total.reshape(4, 16, QC)
        sz_own[ch, h] = total
        sz_tx[ch, h] = total.astype(bf16)
        copies = quad(7, ch, h, lambda to: sz_tx.at[ch, h, to], lambda s: sz_rx.at[ch, h, s], "zh", zh)
        yield
        arrive(copies)
        total = sz_own[ch, h, zh]
        for s in range(3):
            total = total + sz_rx[ch, h, s].astype(f32)
        out_ref[16 * h : 16 * h + 16, lanes] = total

    def step(streams):
        for one in streams:
            next(one, None)

    summed = {}
    first = [[rotate(ch, p) for p in range(2)] for ch in range(CHUNKS)]
    step([first[0][0]])
    rotated(1)
    step([first[0][1], first[1][0], first[1][1]])
    for stage in range(1, 4):
        step(first[0] + first[1])
        if stage == 1:
            loads[3].wait()
            for t in range(8):
                block = at_v[:, t * 128 : (t + 1) * 128].T
                for i in range(4):
                    c = 4 * t + i
                    for h in range(2):
                        at = 32 * i + 16 * h
                        act[c % 2, h, (c // 2) % 4, c // 8] = block[at : at + 16]
    for ch in range(CHUNKS):
        for p in range(2):
            step([first[ch][p]])
            expand(ch, p, summed)
    second = [[collect(ch, p, summed) for p in range(2)] for ch in range(CHUNKS)]
    for stage in range(4):
        step(second[0] + second[1])
    for ch in range(CHUNKS):
        for p in range(2):
            step([second[ch][p]])
            score(ch, p, summed)
    third = [finish(ch, h, summed) for ch in range(CHUNKS) for h in range(2)]
    step(third)
    for copy in sent:
        copy.wait_send()
    sent.clear()
    step(third)
    step(third)
    for copy in sent:
        copy.wait_send()


def per_device(eigenbasis, eigenvalues, queries, activations):
    n = CHUNKS
    dma = pltpu.SemaphoreType.DMA
    V = pltpu.VMEM

    def parts(lanes, *lead):
        return [V((n, *lead, hi - lo), f32) for lo, hi in lanes]

    any_space = pl.BlockSpec(memory_space=pl.ANY)
    vmem = pl.BlockSpec(memory_space=V)
    return pl.pallas_call(
        kernel,
        out_shape=jax.ShapeDtypeStruct((32, 256), f32),
        in_specs=[any_space, vmem, any_space, any_space],
        out_specs=vmem,
        scratch_shapes=[
            V((COLS, 1152), f32), V((1152, 256), f32), V((WIN, 1024), bf16),
            V((COLS, 1152), bf16), V((COLS, 1152), bf16), V((COLS, 256), f32), V((2, 2, 4, 4, 16, WIN), bf16),
            parts(EIG, 4, 32), parts(EIG, 3, 32), parts(EIG, 4, 8), parts(EIG, 3, 8), parts(EIG, 4, 4, 8),
            parts(WIDE, QC), parts(WIDE, QC), parts(WIDE, 4, 32), parts(WIDE, 3, 32), parts(WIDE, 4, 8),
            parts(WIDE, 3, 8), [V((n, 16, w), bf16) for w in PACK], [V((n, 4, 4, 16, w), bf16) for w in PACK],
            V((n, QC, WIN), f32),
            V((n, 2, 256, QC), f32), V((n, 2, 256, QC), f32),
            V((n, 2, 4, 64, QC), bf16), V((n, 2, 4, 64, QC), f32), V((n, 2, 3, 64, QC), bf16),
            V((n, 2, 4, 16, QC), bf16), V((n, 2, 4, 16, QC), f32), V((n, 2, 3, 16, QC), bf16),
            dma((4,)), dma((8, n, 2, 3)), dma((8, n, 2, 3)), dma((2, n)), dma((2, n)), dma((n, 2)), dma((n, 2)),
            dma((2, n)), dma((2, n)), dma((n, 2, 15)), dma((n, 2, 15)),
        ],
        compiler_params=pltpu.CompilerParams(
            collective_id=1, has_side_effects=True, vmem_limit_bytes=56 * 1024 * 1024
        ),
    )(eigenbasis.T, eigenvalues, queries, activations.T)


def solution(mesh):
    placed = (P("row", "col"), P("col"), P("row", None), P("row", "col"))
    return jax.shard_map(
        per_device, mesh=mesh, in_specs=placed, out_specs=P(("row", "col"), None), check_vma=False
    )
```

time: 88.1 us -> 85.3 us (0.968)
  Pallas kernels: 86.5 us -> 83.7 us
    pallas_call x1, Pallas kernels: 86.5 us -> 83.7 us  [per_device(): pl.pallas_call(kernel, out_shape=jax.ShapeDtypeStruct((32, 256), f32), in...]
where the time goes in v3:
time: 85.3 us; the launch traced here: 85.1 us
  Pallas kernels  83.7 us (98%)
  local copies, waits for them, and re-layouts  1.38 us (2%)
    pallas_call x1, Pallas kernels, per_device(): pl.pallas_call(kernel, out_shape=jax.ShapeDtypeStruct((32, 256), f32), in...  83.7 us

profile of v3, /device:TPU:1, one launch (start us, length us, event | category | flops | bytes accessed | tf_op | source)
XLA Modules:
  0.0 85.1 jit_solution(13500187392613726761)
XLA Ops:
  0.0 83.7 %shard_map.46 = f32[32,256]{1,0:T(8,128)} custom-call(f32[576,1152]{1,0:T(8,128)} %bitcast.2, f32[576]{0:T(1024)} %ev_ref.1, f32[1152,256]{1,0:T(8,128)} %q_hbm.1, bf16[576,1024]{1,0:T(8,128)(2,1)} %bitcast.3), custom_call_target="tpu_custom_call" | custom-call | tf_op jit(solution)/shard_map/pallas_call | solution.py:294
  83.7 1.4 %copy.6 = f32[32,256]{1,0:T(8,128)} copy(f32[32,256]{1,0:T(8,128)} %shard_map.46) | data formatting | bytes 65536

commit v4 on v3

--- a/solution.py
+++ b/solution.py
@@ -34,7 +34,7 @@
     ry_tx, ry_rx, rz_tx, rz_rx, st,
     pk_tx, pk_rx, px_tx, px_rx, pz_tx, pz_rx, pm, pc_rx, pc,
     sk_tx, sk_rx, sx_tx, sx_own, sx_rx, sz_tx, sz_own, sz_rx,
-    load_sem, quad_tx, quad_rx, pair_tx, pair_rx, half_tx, half_rx, turn_tx, turn_rx, all_tx, all_rx,
+    load_sem, quad_tx, quad_rx, pair_tx, pair_rx, half_tx, half_rx, turn_tx, turn_rx, all_tx, all_rx, vouched,
 ):
     row, col = lax.axis_index("row"), lax.axis_index("col")
     y, zl = row // 4, row % 4
@@ -65,12 +65,11 @@
         pl.semaphore_signal(barrier, inc=1, device_id=who, device_id_type=MESH)
 
     row_peers = [((y + dy) % 4, (zl + dz) % 4) for dz in (2, 1, 3, 0) for dy in (2, 1, 3, 0)][:15]
-    greet(device(x=from_x, y=zh, zh=from_zh, zl=x))
+    for d in (1, 3):
+        greet(device(zh=(zh + d) % 4))
     for d in (2, 1, 3):
-        greet(device(zh=(zh + d) % 4))
-    for py, pz in row_peers:
-        greet(device(y=py, zl=pz))
-    for d in (2, 1, 3):
+        greet(device(zl=(zl + d) % 4))
+        greet(device(y=(y + d) % 4))
         greet(device(x=(x + d) % 4))
     greet(device(k=1 - k))
 
@@ -89,7 +88,8 @@
         rot[lo:hi, :] = dot(h, qh) + dot(h, ql) + dot(l, qh)
 
     rotated(0)
-    pl.semaphore_wait(barrier, 23)
+    pl.semaphore_wait(barrier, 12)
+    pl.semaphore_signal(vouched, inc=1, device_id=device(zh=(zh + 3) % 4), device_id_type=MESH)
 
     sent = []
 
@@ -259,19 +259,21 @@
                     for h in range(2):
                         at = 32 * i + 16 * h
                         act[c % 2, h, (c // 2) % 4, c // 8] = block[at : at + 16]
+    second = [[collect(ch, p, summed) for p in range(2)] for ch in range(CHUNKS)]
     for ch in range(CHUNKS):
         for p in range(2):
             step([first[ch][p]])
             expand(ch, p, summed)
-    second = [[collect(ch, p, summed) for p in range(2)] for ch in range(CHUNKS)]
-    for stage in range(4):
+        step(second[ch])
+    pl.semaphore_wait(vouched, 1)
+    for stage in range(1, 4):
         step(second[0] + second[1])
+    third = [finish(ch, h, summed) for ch in range(CHUNKS) for h in range(2)]
     for ch in range(CHUNKS):
         for p in range(2):
             step([second[ch][p]])
             score(ch, p, summed)
-    third = [finish(ch, h, summed) for ch in range(CHUNKS) for h in range(2)]
-    step(third)
+        step(third[2 * ch : 2 * ch + 2])
     for copy in sent:
         copy.wait_send()
     sent.clear()
@@ -308,6 +310,7 @@
             V((n, 2, 4, 16, QC), bf16), V((n, 2, 4, 16, QC), f32), V((n, 2, 3, 16, QC), bf16),
             dma((4,)), dma((8, n, 2, 3)), dma((8, n, 2, 3)), dma((2, n)), dma((2, n)), dma((n, 2)), dma((n, 2)),
             dma((2, n)), dma((2, n)), dma((n, 2, 15)), dma((n, 2, 15)),
+            pltpu.SemaphoreType.REGULAR,
         ],
         compiler_params=pltpu.CompilerParams(
             collective_id=1, has_side_effects=True, vmem_limit_bytes=56 * 1024 * 1024

time: 85.3 us -> 83.5 us (0.979)
  Pallas kernels: 83.7 us -> 81.9 us
    pallas_call x1, Pallas kernels: 83.7 us -> 81.9 us  [per_device(): pl.pallas_call(kernel, out_shape=jax.ShapeDtypeStruct((32, 256), f32), in...]
where the time goes in v4:
time: 83.5 us; the launch traced here: 83.3 us
  Pallas kernels  81.9 us (98%)
  local copies, waits for them, and re-layouts  1.38 us (2%)
    pallas_call x1, Pallas kernels, per_device(): pl.pallas_call(kernel, out_shape=jax.ShapeDtypeStruct((32, 256), f32), in...  81.9 us

profile of v4, /device:TPU:1, one launch (start us, length us, event | category | flops | bytes accessed | tf_op | source)
XLA Modules:
  0.0 83.3 jit_solution(14640851298398759950)
XLA Ops:
  0.0 81.9 %shard_map.46 = f32[32,256]{1,0:T(8,128)} custom-call(f32[576,1152]{1,0:T(8,128)} %bitcast.2, f32[576]{0:T(1024)} %ev_ref.1, f32[1152,256]{1,0:T(8,128)} %q_hbm.1, bf16[576,1024]{1,0:T(8,128)(2,1)} %bitcast.3), custom_call_target="tpu_custom_call" | custom-call | tf_op jit(solution)/shard_map/pallas_call | solution.py:296
  81.9 1.4 %copy.6 = f32[32,256]{1,0:T(8,128)} copy(f32[32,256]{1,0:T(8,128)} %shard_map.46) | data formatting | bytes 65536

commit v5 on v4

--- a/solution.py
+++ b/solution.py
@@ -103,7 +103,7 @@
 
     def quad(stage, ch, part, source, target, axis, at):
         copies = []
-        for d in range(1, 4):
+        for d in (2, 1, 3):
             to = (at + d) % 4
             copies.append(
                 send(source(to), target(d - 1), quad_tx.at[stage, ch, part, d - 1], quad_rx.at[stage, ch, part, d - 1],
@@ -239,6 +239,21 @@
             total = total + sz_rx[ch, h, s].astype(f32)
         out_ref[16 * h : 16 * h + 16, lanes] = total
 
+    def lay_tokens():
+        loads[3].wait()
+        for t in range(8):
+            block = at_v[:, t * 128 : (t + 1) * 128].T
+            for i in range(4):
+                c = 4 * t + i
+                for h in range(2):
+                    at = 32 * i + 16 * h
+                    act[c % 2, h, (c // 2) % 4, c // 8] = block[at : at + 16]
+
+    def left():
+        for copy in sent:
+            copy.wait_send()
+        sent.clear()
+
     def step(streams):
         for one in streams:
             next(one, None)
@@ -250,15 +265,6 @@
     step([first[0][1], first[1][0], first[1][1]])
     for stage in range(1, 4):
         step(first[0] + first[1])
-        if stage == 1:
-            loads[3].wait()
-            for t in range(8):
-                block = at_v[:, t * 128 : (t + 1) * 128].T
-                for i in range(4):
-                    c = 4 * t + i
-                    for h in range(2):
-                        at = 32 * i + 16 * h
-                        act[c % 2, h, (c // 2) % 4, c // 8] = block[at : at + 16]
     second = [[collect(ch, p, summed) for p in range(2)] for ch in range(CHUNKS)]
     for ch in range(CHUNKS):
         for p in range(2):
@@ -268,19 +274,18 @@
     pl.semaphore_wait(vouched, 1)
     for stage in range(1, 4):
         step(second[0] + second[1])
+        if stage == 1:
+            lay_tokens()
+            left()
     third = [finish(ch, h, summed) for ch in range(CHUNKS) for h in range(2)]
     for ch in range(CHUNKS):
         for p in range(2):
             step([second[ch][p]])
             score(ch, p, summed)
         step(third[2 * ch : 2 * ch + 2])
-    for copy in sent:
-        copy.wait_send()
-    sent.clear()
     step(third)
+    left()
     step(third)
-    for copy in sent:
-        copy.wait_send()
 
 
 def per_device(eigenbasis, eigenvalues, queries, activations):

time: 83.5 us -> 82.7 us (level)
  no operation moved by 1% of the time
where the time goes in v5:
time: 82.7 us; the launch traced here: 82.5 us
  Pallas kernels  81.1 us (98%)
  local copies, waits for them, and re-layouts  1.38 us (2%)
    pallas_call x1, Pallas kernels, per_device(): pl.pallas_call(kernel, out_shape=jax.ShapeDtypeStruct((32, 256), f32), in...  81.1 us

profile of v5, /device:TPU:1, one launch (start us, length us, event | category | flops | bytes accessed | tf_op | source)
XLA Modules:
  0.0 82.5 jit_solution(14748926388227647695)
XLA Ops:
  0.0 81.1 %shard_map.46 = f32[32,256]{1,0:T(8,128)} custom-call(f32[576,1152]{1,0:T(8,128)} %bitcast.2, f32[576]{0:T(1024)} %ev_ref.1, f32[1152,256]{1,0:T(8,128)} %q_hbm.1, bf16[576,1024]{1,0:T(8,128)(2,1)} %bitcast.3), custom_call_target="tpu_custom_call" | custom-call | tf_op jit(solution)/shard_map/pallas_call | solution.py:301
  81.1 1.4 %copy.6 = f32[32,256]{1,0:T(8,128)} copy(f32[32,256]{1,0:T(8,128)} %shard_map.46) | data formatting | bytes 65536

commit v6 on v5

--- a/solution.py
+++ b/solution.py
@@ -14,8 +14,8 @@
 QC = 128
 COLS = 576
 EIG = ((0, 256), (256, 576))
-WIDE = ((0, 256), (256, 640))
-PACK = (128, 256)
+WIDE = ((0, 384), (384, 640))
+PACK = (256, 128)
 WIN = 640
 
 

time: 82.7 us -> 82.1 us (level)
  no operation moved by 1% of the time
where the time goes in v6:
time: 82.1 us; the launch traced here: 81.9 us
  Pallas kernels  80.5 us (98%)
  local copies, waits for them, and re-layouts  1.38 us (2%)
    pallas_call x1, Pallas kernels, per_device(): pl.pallas_call(kernel, out_shape=jax.ShapeDtypeStruct((32, 256), f32), in...  80.5 us

profile of v6, /device:TPU:1, one launch (start us, length us, event | category | flops | bytes accessed | tf_op | source)
XLA Modules:
  0.0 81.9 jit_solution(2750815220391718653)
XLA Ops:
  0.0 80.5 %shard_map.46 = f32[32,256]{1,0:T(8,128)} custom-call(f32[576,1152]{1,0:T(8,128)} %bitcast.2, f32[576]{0:T(1024)} %ev_ref.1, f32[1152,256]{1,0:T(8,128)} %q_hbm.1, bf16[576,1024]{1,0:T(8,128)(2,1)} %bitcast.3), custom_call_target="tpu_custom_call" | custom-call | tf_op jit(solution)/shard_map/pallas_call | solution.py:301
  80.5 1.4 %copy.6 = f32[32,256]{1,0:T(8,128)} copy(f32[32,256]{1,0:T(8,128)} %shard_map.46) | data formatting | bytes 65536
